TPU v7x, 32 devices: a whole 2x2x4 slice. The times are simulated.
32 devices in a mesh: shuf: 4 (over y, core), key: 8 (over z, x).
Axes of the slice: x: 2, y: 2, z: 4, core: 2. Of those that a mesh axis runs over, the one named last changes fastest.
Arguments:
- embeddings: bfloat16 [4096, 1024], P(('shuf', 'key')), may hold values from -200 to 200
- labels: int32 [4096], P(('shuf', 'key')), may hold values from 0 to 255
- order: int32 [32, 128], P(('shuf', 'key')), may hold values from 0 to 127, each once within a row
- head_weight: bfloat16 [1024, 512], replicated, may hold values from -0.1875 to 0.1875
Outputs:
- grad_embeddings: bfloat16 [4096, 1024], P(('shuf', 'key'))
- grad_head: float32 [1024, 512], P('key')
All inputs are finite; a program needn't handle non-finite values.
Results may differ from a plain program's by a relative error of at most 0.0075.
Values may be sent and summed in bfloat16 or wider, within the bound.
A program may use at most 64 MiB of HBM per device.

v0:
```python
import jax
import jax.numpy as jnp
from jax import lax
from jax.sharding import PartitionSpec as P

exponent_divisor = 0.1
loss_scale = 64.0
epsilon = 1e-06


def tile_terms(query_embeddings, anchor_labels, anchor_index, piece_keys, piece_labels):
    piece_rows = piece_keys.shape[0]
    cosine_score_table = (
        lax.dot_general(
            query_embeddings,
            piece_keys,
            (((1,), (1,)), ((), ())),
            preferred_element_type=jnp.float32,
        )
        / exponent_divisor
    )
    column = jnp.arange(piece_rows, dtype=jnp.int32)
    itself = anchor_index[:, None] == column[None, :]
    exponent = jnp.where(itself, 0.0, jnp.exp(cosine_score_table))
    positive = jnp.logical_and(
        anchor_labels[:, None] == piece_labels[None, :], jnp.logical_not(itself)
    ).astype(jnp.float32)
    return (exponent, positive)


def body(embeddings, labels, order, head_weight):
    row_count = embeddings.shape[0]
    routing = order[0]
    sent_rows = jnp.take(embeddings, routing, axis=0)
    sent_labels = jnp.take(labels, routing, axis=0)
    group_rows, group_labels = (
        lax.all_to_all(sent_rows, "shuf", split_axis=0, concat_axis=0, tiled=True),
        lax.all_to_all(sent_labels, "shuf", split_axis=0, concat_axis=0, tiled=True),
    )
    projected = jnp.dot(group_rows, head_weight, preferred_element_type=jnp.float32)
    row_norm = jnp.sqrt(jnp.sum(projected * projected, axis=1, keepdims=True) + epsilon)
    direction = projected / row_norm
    normed = direction.astype(jnp.bfloat16)
    anchor_index = lax.axis_index("key") * row_count + jnp.arange(row_count, dtype=jnp.int32)
    pieces = (
        lax.all_gather(normed, "key", axis=0, tiled=True),
        lax.all_gather(group_labels, "key", axis=0, tiled=True),
    )
    exponent, positive = tile_terms(normed, group_labels, anchor_index, pieces[0], pieces[1])
    totals = jnp.sum(exponent, axis=1)
    counts = jnp.sum(positive, axis=1)
    floor_count = jnp.maximum(counts, 1.0)
    soft_weight = loss_scale * counts / (floor_count * totals)
    pos_weight = loss_scale / floor_count
    all_soft, all_pos = (
        lax.all_gather(soft_weight, "key", axis=0, tiled=True),
        lax.all_gather(pos_weight, "key", axis=0, tiled=True),
    )
    pieces = (
        lax.all_gather(normed, "key", axis=0, tiled=True),
        lax.all_gather(group_labels, "key", axis=0, tiled=True),
    )
    exponent, positive = tile_terms(normed, group_labels, anchor_index, pieces[0], pieces[1])
    coefficient = (
        (soft_weight[:, None] + all_soft[None, :]) * exponent
        - (pos_weight[:, None] + all_pos[None, :]) * positive
    ).astype(jnp.bfloat16)
    positive_partner = jnp.dot(coefficient, pieces[0], preferred_element_type=jnp.float32)
    positive_pull_derivative = positive_partner / exponent_divisor
    along = jnp.sum(direction * positive_pull_derivative, axis=1, keepdims=True)
    slopes = ((positive_pull_derivative - direction * along) / row_norm).astype(jnp.bfloat16)
    grad_rows = lax.dot_general(
        slopes, head_weight, (((1,), (1,)), ((), ())), preferred_element_type=jnp.float32
    ).astype(jnp.bfloat16)
    returned = lax.all_to_all(grad_rows, "shuf", split_axis=0, concat_axis=0, tiled=True)
    grad_embeddings = jnp.zeros_like(embeddings).at[routing].set(returned)
    summed_all = lax.psum(
        lax.dot_general(
            group_rows, slopes, (((0,), (0,)), ((), ())), preferred_element_type=jnp.float32
        ).astype(jnp.bfloat16),
        "shuf",
    ).astype(jnp.float32)
    grad_head = lax.psum_scatter(summed_all, "key", scatter_dimension=0, tiled=True)
    return (grad_embeddings, grad_head / loss_scale)


def solution(mesh):
    return jax.shard_map(
        body,
        mesh=mesh,
        in_specs=(P(("shuf", "key"), None), P(("shuf", "key")), P(("shuf", "key"), None), P()),
        out_specs=(P(("shuf", "key"), None), P("key", None)),
        check_vma=False,
    )
```

profile of v0, /device:TPU:0, one launch (start us, length us, event | category | flops | bytes accessed | tf_op | source)
XLA Modules:
  0.0 217.9 jit_solution(10399156327444284223)
XLA Ops:
  7.2 0.7 fusion.14
  8.0 0.7 squeeze.9
  8.7 2.0 gather_fusion.1
  10.8 0.1 broadcast_select_fusion
  10.9 10.1 %all_to_all.27 = bf16[4,32,1024]{2,1,0:T(8,128)(2,1)S(1)} all-to-all(bf16[4,32,1024]{2,1,0:T(8,128)(2,1)S(1)} %broadcast_select_fusion), channel_id=1, replica_groups=mesh['shuf'=4,'key'=8] {'shuf'}, dimensions={0} | all-to-all | bytes 524288 | tf_op jit(solution)/shard_map/all_to_all | solution.py:37
  21.0 0.4 multiply_reduce_fusion.1
  21.4 0.8 fusion.16
  22.1 0.6 broadcast.125
  22.7 0.7 reduce.10
  23.4 0.1 squeeze.8
  23.5 1.2 gather_fusion
  24.8 0.1 gather.13
  24.9 0.6 and_select_fusion
  25.4 3.2 %all-to-all-start = ((s32[4,32,1]{1,2,0:T(1,128)}), s32[4,32,1]{1,2,0:T(1,128)S(1)}, u32[]{:S(2)}, u32[]{:S(2)}) async-start(s32[4,32,1]{1,2,0:T(1,128)} %bitcast.2), calls=%async_computation | async-start | bytes 4096 | tf_op jit(solution)/shard_map/all_to_all | solution.py:38
  28.7 3.6 %all-to-all-done = s32[4,32,1]{1,2,0:T(1,128)S(1)} async-done(((s32[4,32,1]{1,2,0:T(1,128)}), s32[4,32,1]{1,2,0:T(1,128)S(1)}, u32[]{:S(2)}, u32[]{:S(2)}) %all-to-all-start) | async-done | bytes 544 | tf_op jit(solution)/shard_map/all_to_all | solution.py:38
  32.4 0.7 reduce.11
  33.1 0.1 eq.14
  33.2 20.7 %all-gather = s32[8,1,128]{2,1,0:T(1,128)S(1)} all-gather(s32[1,1,128]{2,1,0:T(1,128)S(1)} %reshape.148), channel_id=1, replica_groups=mesh['shuf'=4,'key'=8] {'key'}, dimensions={0}, use_global_device_ids=true | all-gather | bytes 4608 | tf_op jit(solution)/shard_map/all_gather | solution.py:47
  53.9 0.3 convert_reduce_fusion
  54.1 8.6 %all-gather.5.cloned.1.call-done = bf16[1024,512]{1,0:T(8,128)(2,1)} async-done(((bf16[128,512]{1,0:T(8,128)(2,1)}), bf16[1024,512]{1,0:T(8,128)(2,1)}) %all-gather.5.cloned.1.call-update) | async-done | bytes 1048592 | tf_op jit(solution)/shard_map/all_gather | solution.py:46
  62.8 1.9 fusion.17
  64.7 18.2 %all-gather.2 = f32[8,1,128]{2,1,0:T(1,128)S(1)} all-gather(f32[1,1,128]{2,1,0:T(1,128)S(1)} %bitcast.36), channel_id=1, replica_groups=mesh['shuf'=4,'key'=8] {'key'}, dimensions={0}, use_global_device_ids=true | all-gather | bytes 4608 | tf_op jit(solution)/shard_map/all_gather | solution.py:57
  82.9 16.1 %all-gather.1 = f32[8,1,128]{2,1,0:T(1,128)S(1)} all-gather(f32[1,1,128]{2,1,0:T(1,128)S(1)} %bitcast.35), channel_id=1, replica_groups=mesh['shuf'=4,'key'=8] {'key'}, dimensions={0}, use_global_device_ids=true | all-gather | bytes 4608 | tf_op jit(solution)/shard_map/all_gather | solution.py:56
  99.1 1.8 multiply_reduce_fusion
  100.8 1.5 convolution_convert_fusion
  102.4 34.9 %all-reduce.2.cloned.1.call-done = bf16[1024,512]{1,0:T(8,128)(2,1)} async-done(((bf16[1024,512]{1,0:T(8,128)(2,1)}), bf16[1024,512]{1,0:T(8,128)(2,1)}) %all-reduce.2.cloned.1.call-update) | async-done | bytes 1048592 | tf_op jit(solution)/shard_map/psum | solution.py:77
  137.3 2.9 %convert_element_type.28 = f32[1024,512]{1,0:T(8,128)} convert(bf16[1024,512]{1,0:T(8,128)(2,1)} %all-reduce.2.cloned.1.call-done) | non-fusion elementwise | flops 524288 | bytes 3145728 | tf_op jit(solution)/shard_map/convert_element_type | solution.py:82
  140.2 0.5 convolution_convert_fusion.1
  140.7 8.4 %all_to_all.28 = bf16[4,32,1024]{2,1,0:T(8,128)(2,1)S(1)} all-to-all(bf16[4,32,1024]{2,1,0:T(8,128)(2,1)S(1)} %bitcast.28), channel_id=1, replica_groups=mesh['shuf'=4,'key'=8] {'shuf'}, dimensions={0} | all-to-all | bytes 524288 | tf_op jit(solution)/shard_map/all_to_all | solution.py:75
  149.2 1.8 scatter_custom_fusion
  151.0 58.7 %reduce-scatter.2.cloned.1.call-done = f32[128,512]{1,0:T(8,128)} async-done(((f32[1024,512]{1,0:T(8,128)}), f32[128,512]{1,0:T(8,128)}) %reduce-scatter.2.cloned.1.call-update) | async-done | bytes 262160 | tf_op jit(solution)/shard_map/reduce_scatter | solution.py:83
  209.7 1.7 broadcast_multiply_fusion
  (18 shorter events, 0.3 us)
Async XLA Ops:
  7.2 13.8 %copy-start = (bf16[1024,512]{1,0:T(8,128)(2,1)S(1)}, bf16[1024,512]{1,0:T(8,128)(2,1)}, u32[]{:S(2)}) copy-start(bf16[1024,512]{1,0:T(8,128)(2,1)} %param.7) | copy-start | bytes 3145732
  7.2 55.6 %all-gather.5.cloned.1.call-start = ((), (), s32[]{:S(2)}) async-start(), calls=%async_computation.4 | async-start | bytes 1179648 | tf_op jit(solution)/shard_map/all_gather | solution.py:46
  10.8 12.0 %copy-start.2 = (s32[1,128]{1,0:T(1,128)S(1)}, s32[1,128]{1,0:T(1,128)}, u32[]{:S(2)}) copy-start(s32[1,128]{1,0:T(1,128)} %param.6) | copy-start | bytes 1540
  10.8 12.8 %copy-start.1 = (s32[128]{0:T(128)S(1)}, s32[128]{0:T(128)}, u32[]{:S(2)}) copy-start(s32[128]{0:T(128)} %param.5) | copy-start | bytes 1540
  25.4 6.9 %all-to-all-start = ((s32[4,32,1]{1,2,0:T(1,128)}), s32[4,32,1]{1,2,0:T(1,128)S(1)}, u32[]{:S(2)}, u32[]{:S(2)}) async-start(s32[4,32,1]{1,2,0:T(1,128)} %bitcast.2), calls=%async_computation | async-start | bytes 4096 | tf_op jit(solution)/shard_map/all_to_all | solution.py:38
  28.7 108.7 %all-reduce.2.cloned.1.call-start = ((), (), s32[]{:S(2)}) async-start(), calls=%async_computation.5 | async-start | bytes 2097152 | tf_op jit(solution)/shard_map/psum | solution.py:77
  102.4 107.3 %reduce-scatter.2.cloned.1.call-start = ((), (), s32[]{:S(2)}) async-start(), calls=%async_computation.6 | async-start | bytes 2359296 | tf_op jit(solution)/shard_map/reduce_scatter | solution.py:83
Sparse Core Ops, SparseCore 0:
  22.3 40.4 all-gather.4
  102.5 34.7 all-reduce.1
  141.3 68.3 reduce-scatter.1
where the time goes:
time: 218 us
  waiting for transfers between devices  106 us (49%)
  blocking collectives  73.6 us (34%)
  between operations  13.8 us (6%)
  other arithmetic  8.45 us (4%)
  local copies, waits for them, and re-layouts  6.74 us (3%)
  matrix products  6.06 us (3%)
  starting transfers between devices  3.34 us (2%)
    reduce_scatter x1, waiting for transfers between devices, body(): lax.psum_scatter(summed_all, 'key', scatter_dimension=0, tiled=True)  58.7 us
    psum x1, waiting for transfers between devices, body(): lax.psum(lax.dot_general(group_rows, slopes, (((0,), (0,)), ((), ())), pr...  34.9 us
    all_gather x1, blocking collectives, body(): lax.all_gather(group_labels, 'key', axis=0, tiled=True)  20.7 us
    all_gather x1, blocking collectives, body(): lax.all_gather(pos_weight, 'key', axis=0, tiled=True)  18.2 us
    all_gather x1, blocking collectives, body(): lax.all_gather(soft_weight, 'key', axis=0, tiled=True)  16.1 us
    all_to_all x1, blocking collectives, body(): lax.all_to_all(sent_rows, 'shuf', split_axis=0, concat_axis=0, tiled=True)  10.1 us
    all_gather x1, waiting for transfers between devices, body(): lax.all_gather(normed, 'key', axis=0, tiled=True)  8.63 us
    all_to_all x1, blocking collectives, body(): lax.all_to_all(grad_rows, 'shuf', split_axis=0, concat_axis=0, tiled=True)  8.42 us
  transfers between devices with their start and end apart: 4, of which 4 were waited for; matrix products, arithmetic and copies ran while one was open for 3% of the time, Pallas kernels for 0%

commit v1 on v0

v1 whole, which is shorter than its diff:
```python
import functools

import jax
import jax.numpy as jnp
from jax import lax
from jax.experimental import pallas as pl
from jax.experimental.pallas import tpu as pltpu
from jax.sharding import PartitionSpec as P

MESH = pl.DeviceIdType.MESH
F32, BF16 = jnp.float32, jnp.bfloat16
exponent_divisor = 0.1
loss_scale = 64.0
epsilon = 1e-06
PARTS = 4


def nn(a, b):
    return lax.dot_general(a, b, (((1,), (0,)), ((), ())), preferred_element_type=F32)


def nt(a, b):
    return lax.dot_general(a, b, (((1,), (1,)), ((), ())), preferred_element_type=F32)


def tn(a, b):
    return lax.dot_general(a, b, (((0,), (0,)), ((), ())), preferred_element_type=F32)


def kernel(
    m, emb_ref, lab_ref, order_ref, head_ref, gemb_ref, ghead_ref,
    slot_ref, group_ref, dir_ref, labs_ref, labz_ref, labg_ref, wts_ref, wtg_ref, exp_ref,
    tan_ref, tanz_ref, alongs_ref, alongz_ref, embt_ref, embg_ref, slq_ref, slg_ref,
    hs_ref, hz_ref, qs_ref, qg_ref,
    zs_sem, zr_sem, lzs_sem, lzr_sem, lgs_sem, lgr_sem, wgs_sem, wgr_sem,
    gs_sem, gr_sem, gfs_sem, gfr_sem, es_sem, er_sem, efs_sem, efr_sem,
    ts_sem, tr_sem, as_sem, ar_sem, ss_sem, sr_sem, hs_sem, hr_sem, qs_sem, qr_sem,
):
    rows, width = emb_ref.shape
    slab = rows // PARTS
    nk = PARTS * m
    dk = width // nk
    quarter = head_ref.shape[1] // PARTS
    u = lax.axis_index("shuf")
    k = lax.axis_index("key")
    z, j = k // m, k % m

    def flip(a, du):
        for bit in (1, 2):
            if du & bit:
                a = a + bit - 2 * bit * ((a // bit) % 2)
        return a

    def ahead(dz):
        return (z + dz) % PARTS

    def behind(dz):
        return (z + PARTS - dz) % PARTS

    def there(du, dj):
        return flip(u, du), (j + dj) % m

    def origin(du, dj):
        return flip(u, du), (j + m - dj) % m

    def block_of(uj):
        return uj[0] * m + uj[1]

    def block_rows(ref, b):
        return ref.at[pl.ds(pl.multiple_of(b * rows, rows), rows)]

    def plane_id(uj):
        return (uj[0], z * m + uj[1])

    def z_id(zz):
        return (u, zz * m + j)

    pending = []

    def send(src, dst, s_sem, r_sem, to):
        copy = pltpu.make_async_remote_copy(
            src_ref=src, dst_ref=dst, send_sem=s_sem, recv_sem=r_sem, device_id=to, device_id_type=MESH
        )
        copy.start()
        pending.append(copy)

    def arrived(dst, s_sem, r_sem, frm):
        pltpu.make_async_remote_copy(
            src_ref=dst, dst_ref=dst, send_sem=s_sem, recv_sem=r_sem, device_id=frm, device_id_type=MESH
        ).wait_recv()

    same_core = [(du, dj) for dj in range(m) for du in (0, 2)]
    plane = [(du, dj) for dj in range(m) for du in range(PARTS)]
    mine = block_of((u, j))

    barrier = pltpu.get_barrier_semaphore()
    for off in plane[1:]:
        pl.semaphore_signal(barrier, inc=1, device_id=plane_id(there(*off)), device_id_type=MESH)
    for dz in range(1, PARTS):
        pl.semaphore_signal(barrier, inc=1, device_id=z_id(ahead(dz)), device_id_type=MESH)

    sub = lax.broadcasted_iota(jnp.int32, (rows, rows), 0)
    lane = lax.broadcasted_iota(jnp.int32, (rows, rows), 1)
    eye = sub == lane
    place = sub == order_ref[...]
    place_bf = place.astype(F32).astype(BF16)

    projected = nn(emb_ref[...], head_ref[...])
    row_norm = jnp.sqrt(jnp.sum(projected * projected, axis=1, keepdims=True) + epsilon)
    direction = projected / row_norm
    dir_ref[...] = direction
    normed = direction.astype(BF16)
    slot_ref[...] = tn(place_bf, normed).astype(BF16)

    def column(row):
        return jnp.sum(jnp.where(eye, row, 0.0), axis=1, keepdims=True)

    def row_of(col):
        return jnp.sum(jnp.where(eye, col, 0.0), axis=0, keepdims=True)

    lab_col = column(lab_ref[...].astype(F32))
    lab_slot = jnp.sum(jnp.where(place, lab_col, 0.0), axis=0, keepdims=True)
    labs_ref[...] = jnp.broadcast_to(lab_slot, labs_ref.shape)
    pl.semaphore_wait(barrier, nk - 1 + PARTS - 1)

    def slab_rows(ref, i):
        return ref.at[pl.ds(pl.multiple_of(i * slab, slab), slab)]

    def group_slab(b, i):
        return group_ref.at[pl.ds(pl.multiple_of(b * rows + i * slab, slab), slab)]

    for dz in range(1, PARTS):
        zz = ahead(dz)
        send(labs_ref, labz_ref.at[z], lzs_sem.at[dz], lzr_sem.at[dz], z_id(zz))
        send(slab_rows(slot_ref, zz), group_slab(mine, z), zs_sem.at[dz], zr_sem.at[dz], z_id(zz))
    own = pl.multiple_of(mine * rows + z * slab, slab)
    group_ref[pl.ds(own, slab), :] = slot_ref[pl.ds(pl.multiple_of(z * slab, slab), slab), :]
    labz_ref[z] = labs_ref[...]

    turned = emb_ref[...].T
    for jj in range(m):
        for zz in range(PARTS):
            first = (zz * m + jj) * dk
            embt_ref[jj, zz * dk : (zz + 1) * dk, :] = turned[first : first + dk, :]
    for i, off in enumerate(same_core):
        if i:
            to = there(*off)
            send(embt_ref.at[to[1]], embg_ref.at[mine], es_sem.at[i], er_sem.at[i], plane_id(to))
    embg_ref[mine] = embt_ref[j]

    def extract(buf_ref):
        lanes = lax.broadcasted_iota(jnp.int32, (8, rows), 1) // slab
        out = jnp.zeros((8, rows), F32)
        for i in range(PARTS):
            moved = pltpu.roll(buf_ref[i], ((i + PARTS - z) % PARTS) * slab, 1)
            out = jnp.where(lanes == i, moved, out)
        return out

    for dz in range(1, PARTS):
        arrived(group_slab(mine, behind(dz)), zs_sem.at[dz], zr_sem.at[dz], z_id(behind(dz)))
    for i, off in enumerate(same_core):
        if i:
            to = there(*off)
            send(block_rows(group_ref, mine), block_rows(group_ref, mine), gs_sem.at[i], gr_sem.at[i], plane_id(to))
    partner = there(1, 0)
    send(block_rows(group_ref, mine), block_rows(group_ref, mine), gfs_sem.at[0], gfr_sem.at[0], plane_id(partner))
    for dz in range(1, PARTS):
        arrived(labz_ref.at[behind(dz)], lzs_sem.at[dz], lzr_sem.at[dz], z_id(behind(dz)))
    labg_ref[mine] = extract(labz_ref)
    for i, off in enumerate(plane):
        if i:
            send(labg_ref.at[mine], labg_ref.at[mine], lgs_sem.at[i], lgr_sem.at[i], plane_id(there(*off)))

    def load_block(b):
        return group_ref[pl.ds(pl.multiple_of(b * rows, rows), rows), :]

    anchors = load_block(mine)
    anchor_col = column(labg_ref[mine][0:1, :])

    def exponent_of(i, b):
        value = jnp.exp(nt(anchors, load_block(b)) / exponent_divisor)
        if i == 0:
            value = jnp.where(eye, 0.0, value)
        exp_ref[i] = value
        return value

    def positive_of(i, b):
        same = anchor_col == labg_ref[b][0:1, :]
        if i == 0:
            same = jnp.logical_and(same, jnp.logical_not(eye))
        return jnp.where(same, 1.0, 0.0)

    total = exponent_of(0, mine)
    blocks = [mine]
    for i, off in enumerate(same_core):
        if i:
            frm = origin(*off)
            b = block_of(frm)
            arrived(block_rows(group_ref, b), gs_sem.at[i], gr_sem.at[i], plane_id(frm))
            send(block_rows(group_ref, b), block_rows(group_ref, b), gfs_sem.at[i], gfr_sem.at[i], plane_id(partner))
            total = total + exponent_of(len(blocks), b)
            blocks.append(b)
    for i, off in enumerate(plane):
        if i:
            frm = origin(*off)
            arrived(labg_ref.at[block_of(frm)], lgs_sem.at[i], lgr_sem.at[i], plane_id(frm))
    forwarded = []
    for i, off in enumerate(same_core):
        uj = origin(*off)
        forwarded.append(block_of((flip(uj[0], 1), uj[1])))
    for i, b in enumerate(forwarded):
        arrived(block_rows(group_ref, b), gfs_sem.at[i], gfr_sem.at[i], plane_id(partner))
        total = total + exponent_of(len(blocks), b)
        blocks.append(b)
    positive = positive_of(0, mine)
    for i in range(1, nk):
        positive = positive + positive_of(i, blocks[i])
    totals = jnp.sum(total, axis=1, keepdims=True)
    counts = jnp.sum(positive, axis=1, keepdims=True)
    floor_count = jnp.maximum(counts, 1.0)
    soft = loss_scale * counts / (floor_count * totals)
    pos = loss_scale / floor_count
    first_row = lax.broadcasted_iota(jnp.int32, (8, rows), 0) == 0
    wts_ref[...] = jnp.where(first_row, row_of(soft), row_of(pos))
    wtg_ref[mine] = wts_ref[...]
    for i, off in enumerate(plane):
        if i:
            send(wts_ref, wtg_ref.at[mine], wgs_sem.at[i], wgr_sem.at[i], plane_id(there(*off)))

    for i, off in enumerate(same_core):
        frm = origin(*off)
        b = block_of(frm)
        if i:
            arrived(embg_ref.at[b], es_sem.at[i], er_sem.at[i], plane_id(frm))
        send(embg_ref.at[b], embg_ref.at[b], efs_sem.at[i], efr_sem.at[i], plane_id(partner))

    for i, off in enumerate(plane):
        if i:
            frm = origin(*off)
            arrived(wtg_ref.at[block_of(frm)], wgs_sem.at[i], wgr_sem.at[i], plane_id(frm))
    pull = jnp.zeros((rows, head_ref.shape[1]), F32)
    for i, b in enumerate(blocks):
        weights = wtg_ref[b]
        coefficient = (soft + weights[0:1, :]) * exp_ref[i] - (pos + weights[1:2, :]) * positive_of(i, b)
        pull = pull + nn(coefficient.astype(BF16), load_block(b))
    pull = pull / exponent_divisor
    anchors32 = anchors.astype(F32)
    along = jnp.sum(anchors32 * pull, axis=1, keepdims=True)
    tan_ref[...] = (pull - anchors32 * along).astype(BF16)
    alongs_ref[...] = jnp.broadcast_to(row_of(along), alongs_ref.shape)
    for dz in range(1, PARTS):
        zz = ahead(dz)
        send(slab_rows(tan_ref, zz), slab_rows(tanz_ref, z), ts_sem.at[dz], tr_sem.at[dz], z_id(zz))
        send(alongs_ref, alongz_ref.at[z], as_sem.at[dz], ar_sem.at[dz], z_id(zz))
    own = pl.multiple_of(z * slab, slab)
    tanz_ref[pl.ds(own, slab), :] = tan_ref[pl.ds(own, slab), :]
    alongz_ref[z] = alongs_ref[...]
    for dz in range(1, PARTS):
        frm = behind(dz)
        arrived(slab_rows(tanz_ref, frm), ts_sem.at[dz], tr_sem.at[dz], z_id(frm))
        arrived(alongz_ref.at[frm], as_sem.at[dz], ar_sem.at[dz], z_id(frm))

    direction = dir_ref[...]
    along = jnp.sum(jnp.where(place, extract(alongz_ref)[0:1, :], 0.0), axis=1, keepdims=True)
    pull = nn(place_bf, tanz_ref[...]) + along * direction.astype(BF16).astype(F32)
    slopes = (pull - direction * jnp.sum(direction * pull, axis=1, keepdims=True)) / row_norm
    slopes = slopes.astype(BF16)
    for uu in range(PARTS):
        slq_ref[uu] = slopes[:, uu * quarter : (uu + 1) * quarter]
    for i, off in enumerate(plane):
        if i:
            to = there(*off)
            send(slq_ref.at[to[0]], slg_ref.at[mine], ss_sem.at[i], sr_sem.at[i], plane_id(to))
    slg_ref[mine] = slq_ref[u]
    gemb_ref[...] = nt(slopes, head_ref[...]).astype(BF16)
    for i, b in enumerate(forwarded):
        arrived(embg_ref.at[b], efs_sem.at[i], efr_sem.at[i], plane_id(partner))
    part = nn(embg_ref[mine], slg_ref[mine])
    for i, off in enumerate(plane):
        if i:
            frm = origin(*off)
            b = block_of(frm)
            arrived(slg_ref.at[b], ss_sem.at[i], sr_sem.at[i], plane_id(frm))
            part = part + nn(embg_ref[b], slg_ref[b])
    hs_ref[...] = part.astype(BF16).reshape(hs_ref.shape)
    for dz in range(1, PARTS):
        zz = ahead(dz)
        send(hs_ref.at[zz], hz_ref.at[z], hs_sem.at[dz], hr_sem.at[dz], z_id(zz))
    hz_ref[z] = hs_ref[z]
    for dz in range(1, PARTS):
        arrived(hz_ref.at[behind(dz)], hs_sem.at[dz], hr_sem.at[dz], z_id(behind(dz)))
    part = hz_ref[0].astype(F32)
    for zz in range(1, PARTS):
        part = part + hz_ref[zz].astype(F32)
    qs_ref[...] = part / loss_scale
    for du in range(1, PARTS):
        send(qs_ref, qg_ref.at[u], qs_sem.at[du], qr_sem.at[du], plane_id(there(du, 0)))
    qg_ref[u] = qs_ref[...]
    for du in range(1, PARTS):
        frm = origin(du, 0)
        arrived(qg_ref.at[frm[0]], qs_sem.at[du], qr_sem.at[du], plane_id(frm))
    for uu in range(PARTS):
        ghead_ref[:, uu * quarter : (uu + 1) * quarter] = qg_ref[uu]
    for copy in pending:
        copy.wait_send()


def body(m, embeddings, labels, order, head_weight):
    rows, width = embeddings.shape
    proj = head_weight.shape[1]
    nk = PARTS * m
    dk = width // nk
    quarter = proj // PARTS
    vmem = pltpu.VMEM
    scratch = [
        vmem((rows, proj), BF16),
        vmem((nk * rows, proj), BF16),
        vmem((rows, proj), F32),
        vmem((8, rows), F32),
        vmem((PARTS, 8, rows), F32),
        vmem((nk, 8, rows), F32),
        vmem((8, rows), F32),
        vmem((nk, 8, rows), F32),
        vmem((nk, rows, rows), F32),
        vmem((rows, proj), BF16),
        vmem((rows, proj), BF16),
        vmem((8, rows), F32),
        vmem((PARTS, 8, rows), F32),
        vmem((m, PARTS * dk, rows), BF16),
        vmem((nk, PARTS * dk, rows), BF16),
        vmem((PARTS, rows, quarter), BF16),
        vmem((nk, rows, quarter), BF16),
        vmem((PARTS, dk, quarter), BF16),
        vmem((PARTS, dk, quarter), BF16),
        vmem((dk, quarter), F32),
        vmem((PARTS, dk, quarter), F32),
    ]
    four, core, full = PARTS, 2 * m, nk
    for count in (four, four, full, full, core, core, core, core, four, four, full, four, four):
        scratch += [pltpu.SemaphoreType.DMA((count,))] * 2
    macs = rows * proj * (2 * width + 2 * nk * rows) + PARTS * dk * nk * rows * quarter
    return pl.pallas_call(
        functools.partial(kernel, m),
        out_shape=(
            jax.ShapeDtypeStruct((rows, width), BF16),
            jax.ShapeDtypeStruct((dk, proj), F32),
        ),
        in_specs=[pl.BlockSpec(memory_space=pltpu.VMEM)] * 4,
        out_specs=(pl.BlockSpec(memory_space=pltpu.VMEM), pl.BlockSpec(memory_space=pltpu.VMEM)),
        scratch_shapes=scratch,
        cost_estimate=pl.CostEstimate(flops=2 * macs, bytes_accessed=4 * rows * width + 2 * width * proj, transcendentals=rows * rows * nk),
        compiler_params=pltpu.CompilerParams(
            collective_id=0, has_side_effects=True, vmem_limit_bytes=48 * 1024 * 1024
        ),
    )(embeddings, labels.reshape(1, rows), order, head_weight)


def solution(mesh):
    m = mesh.shape["key"] // PARTS
    return jax.shard_map(
        functools.partial(body, m),
        mesh=mesh,
        in_specs=(P(("shuf", "key"), None), P(("shuf", "key")), P(("shuf", "key"), None), P()),
        out_specs=(P(("shuf", "key"), None), P("key", None)),
        check_vma=False,
    )
```

time: 218 us -> 47.8 us (0.22)
  waiting for transfers between devices: 106 us -> 0 us
  blocking collectives: 73.6 us -> 0 us
  Pallas kernels: 0 us -> 42.6 us
  between operations: 13.8 us -> 0.66 us
  other arithmetic: 8.45 us -> 0 us
  matrix products: 6.06 us -> 0 us
  starting transfers between devices: 3.34 us -> 0 us
  local copies, waits for them, and re-layouts: 6.74 us -> 4.24 us
    reduce_scatter x1 -> x0, waiting for transfers between devices: 58.7 us -> none  [body(): lax.psum_scatter(summed_all, 'key', scatter_dimension=0, tiled=True)]
    all_gather x3 -> x0, blocking collectives: 55.1 us -> none  [the longest x1 20.7 us: body(): lax.all_gather(group_labels, 'key', axis=0, tiled=True)]
    pallas_call x0 -> x1, Pallas kernels: none -> 42.6 us  [body(): pl.pallas_call(functools.partial(kernel, m), out_shape=(jax.ShapeDtypeStr...]
    psum x1 -> x0, waiting for transfers between devices: 34.9 us -> none  [body(): lax.psum(lax.dot_general(group_rows, slopes, (((0,), (0,)), ((), ())), pr...]
    all_to_all x2 -> x0, blocking collectives: 18.5 us -> none  [the longest x1 10.1 us: body(): lax.all_to_all(sent_rows, 'shuf', split_axis=0, concat_axis=0, tiled=True)]
    all_gather x1 -> x0, waiting for transfers between devices: 8.63 us -> none  [body(): lax.all_gather(normed, 'key', axis=0, tiled=True)]
    dot_general x5 -> x0, matrix products: 6.06 us -> none  [the longest x1 1.89 us: tile_terms(): lax.dot_general(query_embeddings, piece_keys, (((1,), (1,)), ((), ())), p...]
    convert_element_type x2 -> x0, other arithmetic: 3.63 us -> none  [the longest x1 2.87 us: body(): summed_all = lax.psum(lax.dot_general(group_rows, slopes, (((0,), (0,)),...]
  transfers between devices with their start and end apart: 4 -> 0, of which waited for: 4 -> 0; matrix products, arithmetic and copies ran while one was open for 3% -> 0% of each run, Pallas kernels for 0% -> 0%
where the time goes in v1:
time: 47.8 us; the launch traced here: 47.5 us
  Pallas kernels  42.6 us (89%)
  local copies, waits for them, and re-layouts  4.24 us (9%)
  between operations  0.66 us (1%)
    pallas_call x1, Pallas kernels, body(): pl.pallas_call(functools.partial(kernel, m), out_shape=(jax.ShapeDtypeStr...  42.6 us
    unnamed x10, local copies, waits for them, and re-layouts  4.24 us

profile of v1, /device:TPU:0, one launch (start us, length us, event | category | flops | bytes accessed | tf_op | source)
XLA Modules:
  0.0 47.5 jit_solution(1601312511243571928)
XLA Ops:
  0.6 0.0 copy-start.3
  0.6 0.0 copy-start.2
  0.7 0.6 %copy-done.3 = s32[1,128]{1,0:T(1,128)S(1)} copy-done((s32[1,128]{1,0:T(1,128)S(1)}, s32[1,128]{1,0:T(1,128)}, u32[]{:S(2)}) %copy-start.3) | copy-done | bytes 536
  1.3 0.0 copy-done.2
  1.3 0.0 copy-start
  1.3 1.2 %copy-done = bf16[1024,512]{1,0:T(8,128)(2,1)S(1)} copy-done((bf16[1024,512]{1,0:T(8,128)(2,1)S(1)}, bf16[1024,512]{1,0:T(8,128)(2,1)}, u32[]{:S(2)}) %copy-start) | copy-done | bytes 1048600
  2.5 0.0 copy-start.1
  2.5 0.9 %copy-done.1 = bf16[128,1024]{1,0:T(8,128)(2,1)S(1)} copy-done((bf16[128,1024]{1,0:T(8,128)(2,1)S(1)}, bf16[128,1024]{1,0:T(8,128)(2,1)}, u32[]{:S(2)}) %copy-start.1) | copy-done | bytes 262168
  3.5 42.6 %shard_map.59 = (bf16[128,1024]{1,0:T(8,128)(2,1)S(1)}, f32[128,512]{1,0:T(8,128)S(1)}) custom-call(bf16[128,1024]{1,0:T(8,128)(2,1)S(1)} %copy-done.1, s32[1,128]{1,0:T(1,128)S(1)} %bitcast.1, s32[1,128]{1,0:T(1,128)S(1)} %copy-done.3, bf16[1024,512]{1,0:T(8,128)(2,1)S(1)} %copy-done), custom_call_target="tpu_custom_call" | custom-call | flops 671088640 | bytes 1572864 | tf_op jit(solution)/shard_map/pallas_call | solution.py:342
  46.1 0.7 %copy.8 = bf16[128,1024]{1,0:T(8,128)(2,1)} copy(bf16[128,1024]{1,0:T(8,128)(2,1)S(1)} %get-tuple-element.4) | data formatting | bytes 524288
  46.8 0.7 %copy.9 = f32[128,512]{1,0:T(8,128)} copy(f32[128,512]{1,0:T(8,128)S(1)} %get-tuple-element.5) | data formatting | bytes 524288
Async XLA Ops:
  0.6 0.7 %copy-start.3 = (s32[1,128]{1,0:T(1,128)S(1)}, s32[1,128]{1,0:T(1,128)}, u32[]{:S(2)}) copy-start(s32[1,128]{1,0:T(1,128)} %order_ref.1) | copy-start | bytes 1540
  0.6 0.7 %copy-start.2 = (s32[128]{0:T(128)S(1)}, s32[128]{0:T(128)}, u32[]{:S(2)}) copy-start(s32[128]{0:T(128)} %param.5) | copy-start | bytes 1540
  1.3 1.2 %copy-start = (bf16[1024,512]{1,0:T(8,128)(2,1)S(1)}, bf16[1024,512]{1,0:T(8,128)(2,1)}, u32[]{:S(2)}) copy-start(bf16[1024,512]{1,0:T(8,128)(2,1)} %head_ref.1) | copy-start | bytes 3145732
  2.5 0.9 %copy-start.1 = (bf16[128,1024]{1,0:T(8,128)(2,1)S(1)}, bf16[128,1024]{1,0:T(8,128)(2,1)}, u32[]{:S(2)}) copy-start(bf16[128,1024]{1,0:T(8,128)(2,1)} %emb_ref.1) | copy-start | bytes 786436

commit v2 on v1

--- a/solution.py
+++ b/solution.py
@@ -28,13 +28,14 @@
 
 
 def kernel(
-    m, emb_ref, lab_ref, order_ref, head_ref, gemb_ref, ghead_ref,
-    slot_ref, group_ref, dir_ref, labs_ref, labz_ref, labg_ref, wts_ref, wtg_ref, exp_ref,
-    tan_ref, tanz_ref, alongs_ref, alongz_ref, embt_ref, embg_ref, slq_ref, slg_ref,
+    m, emb_hbm, lab_hbm, order_hbm, head_hbm, gemb_ref, ghead_ref,
+    emb_ref, lab_ref, order_ref, head_ref,
+    slot_ref, group_ref, labs_ref, labz_ref, labg_ref, wts_ref, wtg_ref, exp_ref,
+    embs_ref, embz_ref, slope_ref, slopez_ref, embt_ref, embg_ref, slq_ref, slg_ref,
     hs_ref, hz_ref, qs_ref, qg_ref,
-    zs_sem, zr_sem, lzs_sem, lzr_sem, lgs_sem, lgr_sem, wgs_sem, wgr_sem,
+    in_sem, zs_sem, zr_sem, lzs_sem, lzr_sem, lgs_sem, lgr_sem, wgs_sem, wgr_sem,
     gs_sem, gr_sem, gfs_sem, gfr_sem, es_sem, er_sem, efs_sem, efr_sem,
-    ts_sem, tr_sem, as_sem, ar_sem, ss_sem, sr_sem, hs_sem, hr_sem, qs_sem, qr_sem,
+    ts_sem, tr_sem, cs_sem, cr_sem, ss_sem, sr_sem, hs_sem, hr_sem, qs_sem, qr_sem,
 ):
     rows, width = emb_ref.shape
     slab = rows // PARTS
@@ -93,6 +94,14 @@
     plane = [(du, dj) for dj in range(m) for du in range(PARTS)]
     mine = block_of((u, j))
 
+    loads = [
+        pltpu.make_async_copy(src, dst, in_sem.at[i])
+        for i, (src, dst) in enumerate(
+            [(order_hbm, order_ref), (emb_hbm, emb_ref), (lab_hbm, lab_ref), (head_hbm, head_ref)]
+        )
+    ]
+    for load in loads:
+        load.start()
     barrier = pltpu.get_barrier_semaphore()
     for off in plane[1:]:
         pl.semaphore_signal(barrier, inc=1, device_id=plane_id(there(*off)), device_id_type=MESH)
@@ -102,15 +111,20 @@
     sub = lax.broadcasted_iota(jnp.int32, (rows, rows), 0)
     lane = lax.broadcasted_iota(jnp.int32, (rows, rows), 1)
     eye = sub == lane
+    loads[0].wait()
     place = sub == order_ref[...]
     place_bf = place.astype(F32).astype(BF16)
 
-    projected = nn(emb_ref[...], head_ref[...])
-    row_norm = jnp.sqrt(jnp.sum(projected * projected, axis=1, keepdims=True) + epsilon)
-    direction = projected / row_norm
-    dir_ref[...] = direction
-    normed = direction.astype(BF16)
-    slot_ref[...] = tn(place_bf, normed).astype(BF16)
+    def directions(x):
+        projected = nn(x, head_ref[...])
+        row_norm = jnp.sqrt(jnp.sum(projected * projected, axis=1, keepdims=True) + epsilon)
+        return projected / row_norm, row_norm
+
+    loads[1].wait()
+    embs_ref[...] = tn(place_bf, emb_ref[...]).astype(BF16)
+    loads[2].wait()
+    loads[3].wait()
+    slot_ref[...] = directions(embs_ref[...])[0].astype(BF16)
 
     def column(row):
         return jnp.sum(jnp.where(eye, row, 0.0), axis=1, keepdims=True)
@@ -131,22 +145,13 @@
 
     for dz in range(1, PARTS):
         zz = ahead(dz)
-        send(labs_ref, labz_ref.at[z], lzs_sem.at[dz], lzr_sem.at[dz], z_id(zz))
         send(slab_rows(slot_ref, zz), group_slab(mine, z), zs_sem.at[dz], zr_sem.at[dz], z_id(zz))
+    for dz in range(1, PARTS):
+        send(labs_ref, labz_ref.at[z], lzs_sem.at[dz], lzr_sem.at[dz], z_id(ahead(dz)))
     own = pl.multiple_of(mine * rows + z * slab, slab)
-    group_ref[pl.ds(own, slab), :] = slot_ref[pl.ds(pl.multiple_of(z * slab, slab), slab), :]
+    own_slot = pl.multiple_of(z * slab, slab)
+    group_ref[pl.ds(own, slab), :] = slot_ref[pl.ds(own_slot, slab), :]
     labz_ref[z] = labs_ref[...]
-
-    turned = emb_ref[...].T
-    for jj in range(m):
-        for zz in range(PARTS):
-            first = (zz * m + jj) * dk
-            embt_ref[jj, zz * dk : (zz + 1) * dk, :] = turned[first : first + dk, :]
-    for i, off in enumerate(same_core):
-        if i:
-            to = there(*off)
-            send(embt_ref.at[to[1]], embg_ref.at[mine], es_sem.at[i], er_sem.at[i], plane_id(to))
-    embg_ref[mine] = embt_ref[j]
 
     def extract(buf_ref):
         lanes = lax.broadcasted_iota(jnp.int32, (8, rows), 1) // slab
@@ -156,14 +161,20 @@
             out = jnp.where(lanes == i, moved, out)
         return out
 
-    for dz in range(1, PARTS):
-        arrived(group_slab(mine, behind(dz)), zs_sem.at[dz], zr_sem.at[dz], z_id(behind(dz)))
-    for i, off in enumerate(same_core):
-        if i:
-            to = there(*off)
-            send(block_rows(group_ref, mine), block_rows(group_ref, mine), gs_sem.at[i], gr_sem.at[i], plane_id(to))
+    for dz in range(PARTS):
+        piece = group_slab(mine, behind(dz))
+        if dz:
+            arrived(piece, zs_sem.at[dz], zr_sem.at[dz], z_id(behind(dz)))
+        for i, off in enumerate(same_core):
+            if i:
+                n = i * PARTS + dz
+                send(piece, piece, gs_sem.at[n], gr_sem.at[n], plane_id(there(*off)))
     partner = there(1, 0)
     send(block_rows(group_ref, mine), block_rows(group_ref, mine), gfs_sem.at[0], gfr_sem.at[0], plane_id(partner))
+    embz_ref[pl.ds(own_slot, slab), :] = embs_ref[pl.ds(own_slot, slab), :]
+    for dz in range(1, PARTS):
+        zz = ahead(dz)
+        send(slab_rows(embs_ref, zz), slab_rows(embz_ref, z), cs_sem.at[dz], cr_sem.at[dz], z_id(zz))
     for dz in range(1, PARTS):
         arrived(labz_ref.at[behind(dz)], lzs_sem.at[dz], lzr_sem.at[dz], z_id(behind(dz)))
     labg_ref[mine] = extract(labz_ref)
@@ -196,7 +207,9 @@
         if i:
             frm = origin(*off)
             b = block_of(frm)
-            arrived(block_rows(group_ref, b), gs_sem.at[i], gr_sem.at[i], plane_id(frm))
+            for dz in range(PARTS):
+                n = i * PARTS + dz
+                arrived(group_slab(b, behind(dz)), gs_sem.at[n], gr_sem.at[n], plane_id(frm))
             send(block_rows(group_ref, b), block_rows(group_ref, b), gfs_sem.at[i], gfr_sem.at[i], plane_id(partner))
             total = total + exponent_of(len(blocks), b)
             blocks.append(b)
@@ -227,12 +240,20 @@
         if i:
             send(wts_ref, wtg_ref.at[mine], wgs_sem.at[i], wgr_sem.at[i], plane_id(there(*off)))
 
+    for dz in range(1, PARTS):
+        arrived(slab_rows(embz_ref, behind(dz)), cs_sem.at[dz], cr_sem.at[dz], z_id(behind(dz)))
+    turned = embz_ref[...].T
+    for jj in range(m):
+        for zz in range(PARTS):
+            start = (zz * m + jj) * dk
+            embt_ref[jj, zz * dk : (zz + 1) * dk, :] = turned[start : start + dk, :]
     for i, off in enumerate(same_core):
-        frm = origin(*off)
-        b = block_of(frm)
-        if i:
-            arrived(embg_ref.at[b], es_sem.at[i], er_sem.at[i], plane_id(frm))
-        send(embg_ref.at[b], embg_ref.at[b], efs_sem.at[i], efr_sem.at[i], plane_id(partner))
+        if i:
+            to = there(*off)
+            send(embt_ref.at[to[1]], embg_ref.at[mine], es_sem.at[i], er_sem.at[i], plane_id(to))
+    embg_ref[mine] = embt_ref[j]
+    send(embg_ref.at[mine], embg_ref.at[mine], efs_sem.at[0], efr_sem.at[0], plane_id(partner))
+    direction, row_norm = directions(embz_ref[...])
 
     for i, off in enumerate(plane):
         if i:
@@ -244,27 +265,9 @@
         coefficient = (soft + weights[0:1, :]) * exp_ref[i] - (pos + weights[1:2, :]) * positive_of(i, b)
         pull = pull + nn(coefficient.astype(BF16), load_block(b))
     pull = pull / exponent_divisor
-    anchors32 = anchors.astype(F32)
-    along = jnp.sum(anchors32 * pull, axis=1, keepdims=True)
-    tan_ref[...] = (pull - anchors32 * along).astype(BF16)
-    alongs_ref[...] = jnp.broadcast_to(row_of(along), alongs_ref.shape)
-    for dz in range(1, PARTS):
-        zz = ahead(dz)
-        send(slab_rows(tan_ref, zz), slab_rows(tanz_ref, z), ts_sem.at[dz], tr_sem.at[dz], z_id(zz))
-        send(alongs_ref, alongz_ref.at[z], as_sem.at[dz], ar_sem.at[dz], z_id(zz))
-    own = pl.multiple_of(z * slab, slab)
-    tanz_ref[pl.ds(own, slab), :] = tan_ref[pl.ds(own, slab), :]
-    alongz_ref[z] = alongs_ref[...]
-    for dz in range(1, PARTS):
-        frm = behind(dz)
-        arrived(slab_rows(tanz_ref, frm), ts_sem.at[dz], tr_sem.at[dz], z_id(frm))
-        arrived(alongz_ref.at[frm], as_sem.at[dz], ar_sem.at[dz], z_id(frm))
-
-    direction = dir_ref[...]
-    along = jnp.sum(jnp.where(place, extract(alongz_ref)[0:1, :], 0.0), axis=1, keepdims=True)
-    pull = nn(place_bf, tanz_ref[...]) + along * direction.astype(BF16).astype(F32)
     slopes = (pull - direction * jnp.sum(direction * pull, axis=1, keepdims=True)) / row_norm
     slopes = slopes.astype(BF16)
+    slope_ref[...] = slopes
     for uu in range(PARTS):
         slq_ref[uu] = slopes[:, uu * quarter : (uu + 1) * quarter]
     for i, off in enumerate(plane):
@@ -272,7 +275,16 @@
             to = there(*off)
             send(slq_ref.at[to[0]], slg_ref.at[mine], ss_sem.at[i], sr_sem.at[i], plane_id(to))
     slg_ref[mine] = slq_ref[u]
-    gemb_ref[...] = nt(slopes, head_ref[...]).astype(BF16)
+    for dz in range(1, PARTS):
+        zz = ahead(dz)
+        send(slab_rows(slope_ref, zz), slab_rows(slopez_ref, z), ts_sem.at[dz], tr_sem.at[dz], z_id(zz))
+    slopez_ref[pl.ds(own_slot, slab), :] = slope_ref[pl.ds(own_slot, slab), :]
+    for i, off in enumerate(same_core):
+        if i:
+            frm = origin(*off)
+            b = block_of(frm)
+            arrived(embg_ref.at[b], es_sem.at[i], er_sem.at[i], plane_id(frm))
+            send(embg_ref.at[b], embg_ref.at[b], efs_sem.at[i], efr_sem.at[i], plane_id(partner))
     for i, b in enumerate(forwarded):
         arrived(embg_ref.at[b], efs_sem.at[i], efr_sem.at[i], plane_id(partner))
     part = nn(embg_ref[mine], slg_ref[mine])
@@ -288,11 +300,15 @@
         send(hs_ref.at[zz], hz_ref.at[z], hs_sem.at[dz], hr_sem.at[dz], z_id(zz))
     hz_ref[z] = hs_ref[z]
     for dz in range(1, PARTS):
+        frm = behind(dz)
+        arrived(slab_rows(slopez_ref, frm), ts_sem.at[dz], tr_sem.at[dz], z_id(frm))
+    gemb_ref[...] = nt(nn(place_bf, slopez_ref[...]).astype(BF16), head_ref[...]).astype(BF16)
+    for dz in range(1, PARTS):
         arrived(hz_ref.at[behind(dz)], hs_sem.at[dz], hr_sem.at[dz], z_id(behind(dz)))
     part = hz_ref[0].astype(F32)
     for zz in range(1, PARTS):
         part = part + hz_ref[zz].astype(F32)
-    qs_ref[...] = part / loss_scale
+    qs_ref[...] = (part / loss_scale).astype(BF16)
     for du in range(1, PARTS):
         send(qs_ref, qg_ref.at[u], qs_sem.at[du], qr_sem.at[du], plane_id(there(du, 0)))
     qg_ref[u] = qs_ref[...]
@@ -300,7 +316,7 @@
         frm = origin(du, 0)
         arrived(qg_ref.at[frm[0]], qs_sem.at[du], qr_sem.at[du], plane_id(frm))
     for uu in range(PARTS):
-        ghead_ref[:, uu * quarter : (uu + 1) * quarter] = qg_ref[uu]
+        ghead_ref[:, uu * quarter : (uu + 1) * quarter] = qg_ref[uu].astype(F32)
     for copy in pending:
         copy.wait_send()
 
@@ -313,30 +329,34 @@
     quarter = proj // PARTS
     vmem = pltpu.VMEM
     scratch = [
+        vmem((rows, width), BF16),
+        vmem((1, rows), jnp.int32),
+        vmem((1, rows), jnp.int32),
+        vmem((width, proj), BF16),
         vmem((rows, proj), BF16),
         vmem((nk * rows, proj), BF16),
-        vmem((rows, proj), F32),
         vmem((8, rows), F32),
         vmem((PARTS, 8, rows), F32),
         vmem((nk, 8, rows), F32),
         vmem((8, rows), F32),
         vmem((nk, 8, rows), F32),
         vmem((nk, rows, rows), F32),
+        vmem((rows, width), BF16),
+        vmem((rows, width), BF16),
         vmem((rows, proj), BF16),
         vmem((rows, proj), BF16),
-        vmem((8, rows), F32),
-        vmem((PARTS, 8, rows), F32),
         vmem((m, PARTS * dk, rows), BF16),
         vmem((nk, PARTS * dk, rows), BF16),
         vmem((PARTS, rows, quarter), BF16),
         vmem((nk, rows, quarter), BF16),
         vmem((PARTS, dk, quarter), BF16),
         vmem((PARTS, dk, quarter), BF16),
-        vmem((dk, quarter), F32),
-        vmem((PARTS, dk, quarter), F32),
+        vmem((dk, quarter), BF16),
+        vmem((PARTS, dk, quarter), BF16),
+        pltpu.SemaphoreType.DMA((4,)),
     ]
     four, core, full = PARTS, 2 * m, nk
-    for count in (four, four, full, full, core, core, core, core, four, four, full, four, four):
+    for count in (four, four, full, full, core * PARTS, core, core, core, four, four, full, four, four):
         scratch += [pltpu.SemaphoreType.DMA((count,))] * 2
     macs = rows * proj * (2 * width + 2 * nk * rows) + PARTS * dk * nk * rows * quarter
     return pl.pallas_call(
@@ -345,12 +365,12 @@
             jax.ShapeDtypeStruct((rows, width), BF16),
             jax.ShapeDtypeStruct((dk, proj), F32),
         ),
-        in_specs=[pl.BlockSpec(memory_space=pltpu.VMEM)] * 4,
+        in_specs=[pl.BlockSpec(memory_space=pl.ANY)] * 4,
         out_specs=(pl.BlockSpec(memory_space=pltpu.VMEM), pl.BlockSpec(memory_space=pltpu.VMEM)),
         scratch_shapes=scratch,
         cost_estimate=pl.CostEstimate(flops=2 * macs, bytes_accessed=4 * rows * width + 2 * width * proj, transcendentals=rows * rows * nk),
         compiler_params=pltpu.CompilerParams(
-            collective_id=0, has_side_effects=True, vmem_limit_bytes=48 * 1024 * 1024
+            collective_id=0, has_side_effects=True, vmem_limit_bytes=60 * 1024 * 1024
         ),
     )(embeddings, labels.reshape(1, rows), order, head_weight)
 

time: 47.8 us -> 40.7 us (0.85)
  Pallas kernels: 42.6 us -> 37.5 us
  local copies, waits for them, and re-layouts: 4.24 us -> 2.42 us
    pallas_call x1, Pallas kernels: 42.6 us -> 37.5 us  [body(): pl.pallas_call(functools.partial(kernel, m), out_shape=(jax.ShapeDtypeStr...]
    unnamed x10 -> x4, local copies, waits for them, and re-layouts: 4.24 us -> 2.42 us
where the time goes in v2:
time: 40.7 us; the launch traced here: 40.6 us
  Pallas kernels  37.5 us (92%)
  local copies, waits for them, and re-layouts  2.42 us (6%)
  between operations  0.65 us (2%)
    pallas_call x1, Pallas kernels, body(): pl.pallas_call(functools.partial(kernel, m), out_shape=(jax.ShapeDtypeStr...  37.5 us
    unnamed x4, local copies, waits for them, and re-layouts  2.42 us

profile of v2, /device:TPU:0, one launch (start us, length us, event | category | flops | bytes accessed | tf_op | source)
XLA Modules:
  0.0 40.6 jit_solution(13965830757646116289)
XLA Ops:
  0.6 37.5 %shard_map.59 = (bf16[128,1024]{1,0:T(8,128)(2,1)}, f32[128,512]{1,0:T(8,128)}) custom-call(bf16[128,1024]{1,0:T(8,128)(2,1)} %emb_hbm.1, s32[1,128]{1,0:T(1,128)} %bitcast.1, s32[1,128]{1,0:T(1,128)} %order_hbm.1, bf16[1024,512]{1,0:T(8,128)(2,1)} %head_hbm.1), custom_call_target="tpu_custom_call" | custom-call | flops 671088640 | bytes 1572864 | tf_op jit(solution)/shard_map/pallas_call | solution.py:362
  38.1 0.0 copy-start
  38.2 1.7 %copy.8 = bf16[128,1024]{1,0:T(8,128)(2,1)} copy(bf16[128,1024]{1,0:T(8,128)(2,1)} %get-tuple-element.4) | data formatting | bytes 524288
  39.9 0.0 copy-done
  39.9 0.7 %copy.9 = f32[128,512]{1,0:T(8,128)} copy(f32[128,512]{1,0:T(8,128)S(1)} %copy-done) | data formatting | bytes 524288
Async XLA Ops:
  38.1 1.7 %copy-start = (f32[128,512]{1,0:T(8,128)S(1)}, f32[128,512]{1,0:T(8,128)}, u32[]{:S(2)}) copy-start(f32[128,512]{1,0:T(8,128)} %get-tuple-element.5) | copy-start | bytes 786436

commit v3 on v2

--- a/solution.py
+++ b/solution.py
@@ -30,7 +30,7 @@
 def kernel(
     m, emb_hbm, lab_hbm, order_hbm, head_hbm, gemb_ref, ghead_ref,
     emb_ref, lab_ref, order_ref, head_ref,
-    slot_ref, group_ref, labs_ref, labz_ref, labg_ref, wts_ref, wtg_ref, exp_ref,
+    slot_ref, group_ref, labs_ref, labz_ref, labg_ref, wts_ref, wtg_ref, exp_ref, coef_ref,
     embs_ref, embz_ref, slope_ref, slopez_ref, embt_ref, embg_ref, slq_ref, slg_ref,
     hs_ref, hz_ref, qs_ref, qg_ref,
     in_sem, zs_sem, zr_sem, lzs_sem, lzr_sem, lgs_sem, lgr_sem, wgs_sem, wgr_sem,
@@ -70,6 +70,15 @@
     def block_rows(ref, b):
         return ref.at[pl.ds(pl.multiple_of(b * rows, rows), rows)]
 
+    def lanes_of(b):
+        return pl.ds(pl.multiple_of(b * rows, rows), rows)
+
+    def u_rows(ref, uu):
+        return ref[pl.ds(pl.multiple_of(uu * (m * rows), m * rows), m * rows), :]
+
+    def emb_cols(b):
+        return embg_ref.at[b // m, :, lanes_of(b % m)]
+
     def plane_id(uj):
         return (uj[0], z * m + uj[1])
 
@@ -89,6 +98,10 @@
         pltpu.make_async_remote_copy(
             src_ref=dst, dst_ref=dst, send_sem=s_sem, recv_sem=r_sem, device_id=frm, device_id_type=MESH
         ).wait_recv()
+
+    def drain(copies):
+        for copy in copies:
+            copy.wait_send()
 
     same_core = [(du, dj) for dj in range(m) for du in (0, 2)]
     plane = [(du, dj) for dj in range(m) for du in range(PARTS)]
@@ -120,11 +133,10 @@
         row_norm = jnp.sqrt(jnp.sum(projected * projected, axis=1, keepdims=True) + epsilon)
         return projected / row_norm, row_norm
 
+    loads[2].wait()
     loads[1].wait()
-    embs_ref[...] = tn(place_bf, emb_ref[...]).astype(BF16)
-    loads[2].wait()
     loads[3].wait()
-    slot_ref[...] = directions(embs_ref[...])[0].astype(BF16)
+    slot_ref[...] = tn(place_bf, directions(emb_ref[...])[0].astype(BF16)).astype(BF16)
 
     def column(row):
         return jnp.sum(jnp.where(eye, row, 0.0), axis=1, keepdims=True)
@@ -152,6 +164,7 @@
     own_slot = pl.multiple_of(z * slab, slab)
     group_ref[pl.ds(own, slab), :] = slot_ref[pl.ds(own_slot, slab), :]
     labz_ref[z] = labs_ref[...]
+    embs_ref[...] = tn(place_bf, emb_ref[...]).astype(BF16)
 
     def extract(buf_ref):
         lanes = lax.broadcasted_iota(jnp.int32, (8, rows), 1) // slab
@@ -169,76 +182,82 @@
             if i:
                 n = i * PARTS + dz
                 send(piece, piece, gs_sem.at[n], gr_sem.at[n], plane_id(there(*off)))
+        if dz == PARTS - 2:
+            embz_ref[pl.ds(own_slot, slab), :] = embs_ref[pl.ds(own_slot, slab), :]
+            for step in range(1, PARTS):
+                zz = ahead(step)
+                send(slab_rows(embs_ref, zz), slab_rows(embz_ref, z), cs_sem.at[step], cr_sem.at[step], z_id(zz))
     partner = there(1, 0)
     send(block_rows(group_ref, mine), block_rows(group_ref, mine), gfs_sem.at[0], gfr_sem.at[0], plane_id(partner))
-    embz_ref[pl.ds(own_slot, slab), :] = embs_ref[pl.ds(own_slot, slab), :]
-    for dz in range(1, PARTS):
-        zz = ahead(dz)
-        send(slab_rows(embs_ref, zz), slab_rows(embz_ref, z), cs_sem.at[dz], cr_sem.at[dz], z_id(zz))
     for dz in range(1, PARTS):
         arrived(labz_ref.at[behind(dz)], lzs_sem.at[dz], lzr_sem.at[dz], z_id(behind(dz)))
-    labg_ref[mine] = extract(labz_ref)
+    own_label = extract(labz_ref)
+    labg_ref[:, lanes_of(mine)] = own_label
     for i, off in enumerate(plane):
         if i:
-            send(labg_ref.at[mine], labg_ref.at[mine], lgs_sem.at[i], lgr_sem.at[i], plane_id(there(*off)))
-
-    def load_block(b):
-        return group_ref[pl.ds(pl.multiple_of(b * rows, rows), rows), :]
-
-    anchors = load_block(mine)
-    anchor_col = column(labg_ref[mine][0:1, :])
-
-    def exponent_of(i, b):
-        value = jnp.exp(nt(anchors, load_block(b)) / exponent_divisor)
-        if i == 0:
-            value = jnp.where(eye, 0.0, value)
-        exp_ref[i] = value
-        return value
-
-    def positive_of(i, b):
-        same = anchor_col == labg_ref[b][0:1, :]
-        if i == 0:
-            same = jnp.logical_and(same, jnp.logical_not(eye))
+            send(labg_ref.at[:, lanes_of(mine)], labg_ref.at[:, lanes_of(mine)], lgs_sem.at[i], lgr_sem.at[i], plane_id(there(*off)))
+
+    anchors = group_ref[pl.ds(pl.multiple_of(mine * rows, rows), rows), :]
+    anchor_col = column(own_label[0:1, :])
+    wide = m * rows
+    row_id = lax.broadcasted_iota(jnp.int32, (rows, wide), 0) + mine * rows
+    lane_id = lax.broadcasted_iota(jnp.int32, (rows, wide), 1)
+
+    def exponent_of(uu, own):
+        value = jnp.exp(nt(anchors, u_rows(group_ref, uu)) / exponent_divisor)
+        if own:
+            value = jnp.where(row_id == lane_id + uu * wide, 0.0, value)
+        exp_ref[uu] = value
+        return jnp.sum(value, axis=1, keepdims=True)
+
+    def positive_of(uu):
+        same = jnp.logical_and(
+            anchor_col == labg_ref[0:1, uu * wide : (uu + 1) * wide], row_id != lane_id + uu * wide
+        )
         return jnp.where(same, 1.0, 0.0)
 
-    total = exponent_of(0, mine)
-    blocks = [mine]
-    for i, off in enumerate(same_core):
+    def gathered(du):
+        for i, off in enumerate(same_core):
+            if i and off[0] == du:
+                frm = origin(*off)
+                b = block_of(frm)
+                for dz in range(PARTS):
+                    n = i * PARTS + dz
+                    arrived(group_slab(b, behind(dz)), gs_sem.at[n], gr_sem.at[n], plane_id(frm))
+                send(block_rows(group_ref, b), block_rows(group_ref, b), gfs_sem.at[i], gfr_sem.at[i], plane_id(partner))
+
+    def forwarded(du):
+        for i, off in enumerate(same_core):
+            if off[0] == du:
+                uj = origin(*off)
+                b = block_of((flip(uj[0], 1), uj[1]))
+                yield i, b
+
+    gathered(0)
+    total = exponent_of(u, True)
+    gathered(2)
+    total = total + exponent_of(flip(u, 2), False)
+    for i, off in enumerate(plane):
         if i:
             frm = origin(*off)
-            b = block_of(frm)
-            for dz in range(PARTS):
-                n = i * PARTS + dz
-                arrived(group_slab(b, behind(dz)), gs_sem.at[n], gr_sem.at[n], plane_id(frm))
-            send(block_rows(group_ref, b), block_rows(group_ref, b), gfs_sem.at[i], gfr_sem.at[i], plane_id(partner))
-            total = total + exponent_of(len(blocks), b)
-            blocks.append(b)
-    for i, off in enumerate(plane):
-        if i:
-            frm = origin(*off)
-            arrived(labg_ref.at[block_of(frm)], lgs_sem.at[i], lgr_sem.at[i], plane_id(frm))
-    forwarded = []
-    for i, off in enumerate(same_core):
-        uj = origin(*off)
-        forwarded.append(block_of((flip(uj[0], 1), uj[1])))
-    for i, b in enumerate(forwarded):
-        arrived(block_rows(group_ref, b), gfs_sem.at[i], gfr_sem.at[i], plane_id(partner))
-        total = total + exponent_of(len(blocks), b)
-        blocks.append(b)
-    positive = positive_of(0, mine)
-    for i in range(1, nk):
-        positive = positive + positive_of(i, blocks[i])
-    totals = jnp.sum(total, axis=1, keepdims=True)
-    counts = jnp.sum(positive, axis=1, keepdims=True)
+            arrived(labg_ref.at[:, lanes_of(block_of(frm))], lgs_sem.at[i], lgr_sem.at[i], plane_id(frm))
+    counts = jnp.sum(positive_of(0), axis=1, keepdims=True)
+    for uu in range(1, PARTS):
+        counts = counts + jnp.sum(positive_of(uu), axis=1, keepdims=True)
+    for du in (0, 2):
+        for i, b in forwarded(du):
+            arrived(block_rows(group_ref, b), gfs_sem.at[i], gfr_sem.at[i], plane_id(partner))
+        total = total + exponent_of(flip(u, du + 1), False)
+    totals = total
     floor_count = jnp.maximum(counts, 1.0)
     soft = loss_scale * counts / (floor_count * totals)
     pos = loss_scale / floor_count
     first_row = lax.broadcasted_iota(jnp.int32, (8, rows), 0) == 0
     wts_ref[...] = jnp.where(first_row, row_of(soft), row_of(pos))
-    wtg_ref[mine] = wts_ref[...]
+    wtg_ref[:, lanes_of(mine)] = wts_ref[...]
     for i, off in enumerate(plane):
         if i:
-            send(wts_ref, wtg_ref.at[mine], wgs_sem.at[i], wgr_sem.at[i], plane_id(there(*off)))
+            send(wts_ref, wtg_ref.at[:, lanes_of(mine)], wgs_sem.at[i], wgr_sem.at[i], plane_id(there(*off)))
 
     for dz in range(1, PARTS):
         arrived(slab_rows(embz_ref, behind(dz)), cs_sem.at[dz], cr_sem.at[dz], z_id(behind(dz)))
@@ -250,21 +269,20 @@
     for i, off in enumerate(same_core):
         if i:
             to = there(*off)
-            send(embt_ref.at[to[1]], embg_ref.at[mine], es_sem.at[i], er_sem.at[i], plane_id(to))
-    embg_ref[mine] = embt_ref[j]
-    send(embg_ref.at[mine], embg_ref.at[mine], efs_sem.at[0], efr_sem.at[0], plane_id(partner))
+            send(embt_ref.at[to[1]], emb_cols(mine), es_sem.at[i], er_sem.at[i], plane_id(to))
+    embg_ref[u, :, lanes_of(j)] = embt_ref[j]
+    send(emb_cols(mine), emb_cols(mine), efs_sem.at[0], efr_sem.at[0], plane_id(partner))
     direction, row_norm = directions(embz_ref[...])
 
     for i, off in enumerate(plane):
         if i:
             frm = origin(*off)
-            arrived(wtg_ref.at[block_of(frm)], wgs_sem.at[i], wgr_sem.at[i], plane_id(frm))
-    pull = jnp.zeros((rows, head_ref.shape[1]), F32)
-    for i, b in enumerate(blocks):
-        weights = wtg_ref[b]
-        coefficient = (soft + weights[0:1, :]) * exp_ref[i] - (pos + weights[1:2, :]) * positive_of(i, b)
-        pull = pull + nn(coefficient.astype(BF16), load_block(b))
-    pull = pull / exponent_divisor
+            arrived(wtg_ref.at[:, lanes_of(block_of(frm))], wgs_sem.at[i], wgr_sem.at[i], plane_id(frm))
+    for uu in range(PARTS):
+        cols = slice(uu * wide, (uu + 1) * wide)
+        coefficient = (soft + wtg_ref[0:1, cols]) * exp_ref[uu] - (pos + wtg_ref[1:2, cols]) * positive_of(uu)
+        coef_ref[:, cols] = coefficient.astype(BF16)
+    pull = nn(coef_ref[...], group_ref[...]) / exponent_divisor
     slopes = (pull - direction * jnp.sum(direction * pull, axis=1, keepdims=True)) / row_norm
     slopes = slopes.astype(BF16)
     slope_ref[...] = slopes
@@ -273,8 +291,8 @@
     for i, off in enumerate(plane):
         if i:
             to = there(*off)
-            send(slq_ref.at[to[0]], slg_ref.at[mine], ss_sem.at[i], sr_sem.at[i], plane_id(to))
-    slg_ref[mine] = slq_ref[u]
+            send(slq_ref.at[to[0]], block_rows(slg_ref, mine), ss_sem.at[i], sr_sem.at[i], plane_id(to))
+    slg_ref[pl.ds(pl.multiple_of(mine * rows, rows), rows), :] = slq_ref[u]
     for dz in range(1, PARTS):
         zz = ahead(dz)
         send(slab_rows(slope_ref, zz), slab_rows(slopez_ref, z), ts_sem.at[dz], tr_sem.at[dz], z_id(zz))
@@ -283,17 +301,20 @@
         if i:
             frm = origin(*off)
             b = block_of(frm)
-            arrived(embg_ref.at[b], es_sem.at[i], er_sem.at[i], plane_id(frm))
-            send(embg_ref.at[b], embg_ref.at[b], efs_sem.at[i], efr_sem.at[i], plane_id(partner))
-    for i, b in enumerate(forwarded):
-        arrived(embg_ref.at[b], efs_sem.at[i], efr_sem.at[i], plane_id(partner))
-    part = nn(embg_ref[mine], slg_ref[mine])
-    for i, off in enumerate(plane):
-        if i:
-            frm = origin(*off)
-            b = block_of(frm)
-            arrived(slg_ref.at[b], ss_sem.at[i], sr_sem.at[i], plane_id(frm))
-            part = part + nn(embg_ref[b], slg_ref[b])
+            arrived(emb_cols(b), es_sem.at[i], er_sem.at[i], plane_id(frm))
+            send(emb_cols(b), emb_cols(b), efs_sem.at[i], efr_sem.at[i], plane_id(partner))
+    part = None
+    for du in range(PARTS):
+        if du % 2:
+            for i, b in forwarded(du - 1):
+                arrived(emb_cols(b), efs_sem.at[i], efr_sem.at[i], plane_id(partner))
+        for i, off in enumerate(plane):
+            if i and off[0] == du:
+                frm = origin(*off)
+                arrived(block_rows(slg_ref, block_of(frm)), ss_sem.at[i], sr_sem.at[i], plane_id(frm))
+        term = nn(embg_ref[flip(u, du)], u_rows(slg_ref, flip(u, du)))
+        part = term if part is None else part + term
+    earlier = len(pending)
     hs_ref[...] = part.astype(BF16).reshape(hs_ref.shape)
     for dz in range(1, PARTS):
         zz = ahead(dz)
@@ -302,6 +323,7 @@
     for dz in range(1, PARTS):
         frm = behind(dz)
         arrived(slab_rows(slopez_ref, frm), ts_sem.at[dz], tr_sem.at[dz], z_id(frm))
+    drain(pending[:earlier])
     gemb_ref[...] = nt(nn(place_bf, slopez_ref[...]).astype(BF16), head_ref[...]).astype(BF16)
     for dz in range(1, PARTS):
         arrived(hz_ref.at[behind(dz)], hs_sem.at[dz], hr_sem.at[dz], z_id(behind(dz)))
@@ -317,8 +339,7 @@
         arrived(qg_ref.at[frm[0]], qs_sem.at[du], qr_sem.at[du], plane_id(frm))
     for uu in range(PARTS):
         ghead_ref[:, uu * quarter : (uu + 1) * quarter] = qg_ref[uu].astype(F32)
-    for copy in pending:
-        copy.wait_send()
+    drain(pending[earlier:])
 
 
 def body(m, embeddings, labels, order, head_weight):
@@ -337,18 +358,19 @@
         vmem((nk * rows, proj), BF16),
         vmem((8, rows), F32),
         vmem((PARTS, 8, rows), F32),
-        vmem((nk, 8, rows), F32),
+        vmem((8, nk * rows), F32),
         vmem((8, rows), F32),
-        vmem((nk, 8, rows), F32),
-        vmem((nk, rows, rows), F32),
+        vmem((8, nk * rows), F32),
+        vmem((PARTS, rows, m * rows), F32),
+        vmem((rows, nk * rows), BF16),
         vmem((rows, width), BF16),
         vmem((rows, width), BF16),
         vmem((rows, proj), BF16),
         vmem((rows, proj), BF16),
         vmem((m, PARTS * dk, rows), BF16),
-        vmem((nk, PARTS * dk, rows), BF16),
+        vmem((PARTS, PARTS * dk, m * rows), BF16),
         vmem((PARTS, rows, quarter), BF16),
-        vmem((nk, rows, quarter), BF16),
+        vmem((nk * rows, quarter), BF16),
         vmem((PARTS, dk, quarter), BF16),
         vmem((PARTS, dk, quarter), BF16),
         vmem((dk, quarter), BF16),
@@ -365,12 +387,12 @@
             jax.ShapeDtypeStruct((rows, width), BF16),
             jax.ShapeDtypeStruct((dk, proj), F32),
         ),
-        in_specs=[pl.BlockSpec(memory_space=pl.ANY)] * 4,
+        in_specs=[pl.BlockSpec(memory_space=pltpu.HBM)] * 4,
         out_specs=(pl.BlockSpec(memory_space=pltpu.VMEM), pl.BlockSpec(memory_space=pltpu.VMEM)),
         scratch_shapes=scratch,
         cost_estimate=pl.CostEstimate(flops=2 * macs, bytes_accessed=4 * rows * width + 2 * width * proj, transcendentals=rows * rows * nk),
         compiler_params=pltpu.CompilerParams(
-            collective_id=0, has_side_effects=True, vmem_limit_bytes=60 * 1024 * 1024
+            collective_id=0, has_side_effects=True, vmem_limit_bytes=32 * 1024 * 1024
         ),
     )(embeddings, labels.reshape(1, rows), order, head_weight)
 

time: 40.7 us -> 42 us (1.032)
  local copies, waits for them, and re-layouts: 2.42 us -> 4.24 us
  Pallas kernels: 37.5 us -> 37 us
    unnamed x4 -> x10, local copies, waits for them, and re-layouts: 2.42 us -> 4.24 us
    pallas_call x1, Pallas kernels: 37.5 us -> 37 us  [body(): pl.pallas_call(functools.partial(kernel, m), out_shape=(jax.ShapeDtypeStr...]
where the time goes in v3:
time: 42 us; the launch traced here: 41.9 us
  Pallas kernels  37 us (88%)
  local copies, waits for them, and re-layouts  4.24 us (10%)
  between operations  0.66 us (2%)
    pallas_call x1, Pallas kernels, body(): pl.pallas_call(functools.partial(kernel, m), out_shape=(jax.ShapeDtypeStr...  37 us
    unnamed x10, local copies, waits for them, and re-layouts  4.24 us

profile of v3, /device:TPU:0, one launch (start us, length us, event | category | flops | bytes accessed | tf_op | source)
XLA Modules:
  0.0 41.9 jit_solution(3804723390505663440)
XLA Ops:
  0.6 0.0 copy-start.3
  0.6 0.0 copy-start.2
  0.7 0.6 %copy-done.3 = s32[1,128]{1,0:T(1,128)S(1)} copy-done((s32[1,128]{1,0:T(1,128)S(1)}, s32[1,128]{1,0:T(1,128)}, u32[]{:S(2)}) %copy-start.3) | copy-done | bytes 536
  1.3 0.0 copy-done.2
  1.3 0.0 copy-start
  1.3 1.2 %copy-done = bf16[1024,512]{1,0:T(8,128)(2,1)S(1)} copy-done((bf16[1024,512]{1,0:T(8,128)(2,1)S(1)}, bf16[1024,512]{1,0:T(8,128)(2,1)}, u32[]{:S(2)}) %copy-start) | copy-done | bytes 1048600
  2.5 0.0 copy-start.1
  2.5 0.9 %copy-done.1 = bf16[128,1024]{1,0:T(8,128)(2,1)S(1)} copy-done((bf16[128,1024]{1,0:T(8,128)(2,1)S(1)}, bf16[128,1024]{1,0:T(8,128)(2,1)}, u32[]{:S(2)}) %copy-start.1) | copy-done | bytes 262168
  3.5 37.0 %shard_map.59 = (bf16[128,1024]{1,0:T(8,128)(2,1)S(1)}, f32[128,512]{1,0:T(8,128)S(1)}) custom-call(bf16[128,1024]{1,0:T(8,128)(2,1)S(1)} %copy-done.1, s32[1,128]{1,0:T(1,128)S(1)} %bitcast.1, s32[1,128]{1,0:T(1,128)S(1)} %copy-done.3, bf16[1024,512]{1,0:T(8,128)(2,1)S(1)} %copy-done), custom_call_target="tpu_custom_call" | custom-call | flops 671088640 | bytes 1572864 | tf_op jit(solution)/shard_map/pallas_call | solution.py:384
  40.4 0.7 %copy.8 = bf16[128,1024]{1,0:T(8,128)(2,1)} copy(bf16[128,1024]{1,0:T(8,128)(2,1)S(1)} %get-tuple-element.4) | data formatting | bytes 524288
  41.2 0.7 %copy.9 = f32[128,512]{1,0:T(8,128)} copy(f32[128,512]{1,0:T(8,128)S(1)} %get-tuple-element.5) | data formatting | bytes 524288
Async XLA Ops:
  0.6 0.7 %copy-start.3 = (s32[1,128]{1,0:T(1,128)S(1)}, s32[1,128]{1,0:T(1,128)}, u32[]{:S(2)}) copy-start(s32[1,128]{1,0:T(1,128)} %order_hbm.1) | copy-start | bytes 1540
  0.6 0.7 %copy-start.2 = (s32[128]{0:T(128)S(1)}, s32[128]{0:T(128)}, u32[]{:S(2)}) copy-start(s32[128]{0:T(128)} %param.5) | copy-start | bytes 1540
  1.3 1.2 %copy-start = (bf16[1024,512]{1,0:T(8,128)(2,1)S(1)}, bf16[1024,512]{1,0:T(8,128)(2,1)}, u32[]{:S(2)}) copy-start(bf16[1024,512]{1,0:T(8,128)(2,1)} %head_hbm.1) | copy-start | bytes 3145732
  2.5 0.9 %copy-start.1 = (bf16[128,1024]{1,0:T(8,128)(2,1)S(1)}, bf16[128,1024]{1,0:T(8,128)(2,1)}, u32[]{:S(2)}) copy-start(bf16[128,1024]{1,0:T(8,128)(2,1)} %emb_hbm.1) | copy-start | bytes 786436

commit v4 on v3

--- a/solution.py
+++ b/solution.py
@@ -165,6 +165,10 @@
     group_ref[pl.ds(own, slab), :] = slot_ref[pl.ds(own_slot, slab), :]
     labz_ref[z] = labs_ref[...]
     embs_ref[...] = tn(place_bf, emb_ref[...]).astype(BF16)
+    embz_ref[pl.ds(own_slot, slab), :] = embs_ref[pl.ds(own_slot, slab), :]
+    for dz in range(1, PARTS):
+        zz = ahead(dz)
+        send(slab_rows(embs_ref, zz), slab_rows(embz_ref, z), cs_sem.at[dz], cr_sem.at[dz], z_id(zz))
 
     def extract(buf_ref):
         lanes = lax.broadcasted_iota(jnp.int32, (8, rows), 1) // slab
@@ -182,11 +186,6 @@
             if i:
                 n = i * PARTS + dz
                 send(piece, piece, gs_sem.at[n], gr_sem.at[n], plane_id(there(*off)))
-        if dz == PARTS - 2:
-            embz_ref[pl.ds(own_slot, slab), :] = embs_ref[pl.ds(own_slot, slab), :]
-            for step in range(1, PARTS):
-                zz = ahead(step)
-                send(slab_rows(embs_ref, zz), slab_rows(embz_ref, z), cs_sem.at[step], cr_sem.at[step], z_id(zz))
     partner = there(1, 0)
     send(block_rows(group_ref, mine), block_rows(group_ref, mine), gfs_sem.at[0], gfr_sem.at[0], plane_id(partner))
     for dz in range(1, PARTS):
@@ -392,7 +391,7 @@
         scratch_shapes=scratch,
         cost_estimate=pl.CostEstimate(flops=2 * macs, bytes_accessed=4 * rows * width + 2 * width * proj, transcendentals=rows * rows * nk),
         compiler_params=pltpu.CompilerParams(
-            collective_id=0, has_side_effects=True, vmem_limit_bytes=32 * 1024 * 1024
+            collective_id=0, has_side_effects=True, vmem_limit_bytes=60 * 1024 * 1024
         ),
     )(embeddings, labels.reshape(1, rows), order, head_weight)
 

time: 42 us -> 41.8 us (level)
  local copies, waits for them, and re-layouts: 4.24 us -> 2.42 us
  Pallas kernels: 37 us -> 38.6 us
    unnamed x10 -> x4, local copies, waits for them, and re-layouts: 4.24 us -> 2.42 us
    pallas_call x1, Pallas kernels: 37 us -> 38.6 us  [body(): pl.pallas_call(functools.partial(kernel, m), out_shape=(jax.ShapeDtypeStr...]
where the time goes in v4:
time: 41.8 us; the launch traced here: 41.6 us
  Pallas kernels  38.6 us (92%)
  local copies, waits for them, and re-layouts  2.42 us (6%)
  between operations  0.65 us (2%)
    pallas_call x1, Pallas kernels, body(): pl.pallas_call(functools.partial(kernel, m), out_shape=(jax.ShapeDtypeStr...  38.6 us
    unnamed x4, local copies, waits for them, and re-layouts  2.42 us

profile of v4, /device:TPU:0, one launch (start us, length us, event | category | flops | bytes accessed | tf_op | source)
XLA Modules:
  0.0 41.6 jit_solution(2907880492670364764)
XLA Ops:
  0.6 38.6 %shard_map.59 = (bf16[128,1024]{1,0:T(8,128)(2,1)}, f32[128,512]{1,0:T(8,128)}) custom-call(bf16[128,1024]{1,0:T(8,128)(2,1)} %emb_hbm.1, s32[1,128]{1,0:T(1,128)} %bitcast.1, s32[1,128]{1,0:T(1,128)} %order_hbm.1, bf16[1024,512]{1,0:T(8,128)(2,1)} %head_hbm.1), custom_call_target="tpu_custom_call" | custom-call | flops 671088640 | bytes 1572864 | tf_op jit(solution)/shard_map/pallas_call | solution.py:383
  39.2 0.0 copy-start
  39.2 1.7 %copy.8 = bf16[128,1024]{1,0:T(8,128)(2,1)} copy(bf16[128,1024]{1,0:T(8,128)(2,1)} %get-tuple-element.4) | data formatting | bytes 524288
  40.9 0.0 copy-done
  40.9 0.7 %copy.9 = f32[128,512]{1,0:T(8,128)} copy(f32[128,512]{1,0:T(8,128)S(1)} %copy-done) | data formatting | bytes 524288
Async XLA Ops:
  39.2 1.7 %copy-start = (f32[128,512]{1,0:T(8,128)S(1)}, f32[128,512]{1,0:T(8,128)}, u32[]{:S(2)}) copy-start(f32[128,512]{1,0:T(8,128)} %get-tuple-element.5) | copy-start | bytes 786436

commit v5 on v3

--- a/solution.py
+++ b/solution.py
@@ -164,7 +164,6 @@
     own_slot = pl.multiple_of(z * slab, slab)
     group_ref[pl.ds(own, slab), :] = slot_ref[pl.ds(own_slot, slab), :]
     labz_ref[z] = labs_ref[...]
-    embs_ref[...] = tn(place_bf, emb_ref[...]).astype(BF16)
 
     def extract(buf_ref):
         lanes = lax.broadcasted_iota(jnp.int32, (8, rows), 1) // slab
@@ -182,11 +181,12 @@
             if i:
                 n = i * PARTS + dz
                 send(piece, piece, gs_sem.at[n], gr_sem.at[n], plane_id(there(*off)))
-        if dz == PARTS - 2:
+        if dz == 0:
+            embs_ref[...] = tn(place_bf, emb_ref[...]).astype(BF16)
             embz_ref[pl.ds(own_slot, slab), :] = embs_ref[pl.ds(own_slot, slab), :]
-            for step in range(1, PARTS):
-                zz = ahead(step)
-                send(slab_rows(embs_ref, zz), slab_rows(embz_ref, z), cs_sem.at[step], cr_sem.at[step], z_id(zz))
+    for dz in range(1, PARTS):
+        zz = ahead(dz)
+        send(slab_rows(embs_ref, zz), slab_rows(embz_ref, z), cs_sem.at[dz], cr_sem.at[dz], z_id(zz))
     partner = there(1, 0)
     send(block_rows(group_ref, mine), block_rows(group_ref, mine), gfs_sem.at[0], gfr_sem.at[0], plane_id(partner))
     for dz in range(1, PARTS):
@@ -234,8 +234,8 @@
                 yield i, b
 
     gathered(0)
+    gathered(2)
     total = exponent_of(u, True)
-    gathered(2)
     total = total + exponent_of(flip(u, 2), False)
     for i, off in enumerate(plane):
         if i:
@@ -392,7 +392,7 @@
         scratch_shapes=scratch,
         cost_estimate=pl.CostEstimate(flops=2 * macs, bytes_accessed=4 * rows * width + 2 * width * proj, transcendentals=rows * rows * nk),
         compiler_params=pltpu.CompilerParams(
-            collective_id=0, has_side_effects=True, vmem_limit_bytes=32 * 1024 * 1024
+            collective_id=0, has_side_effects=True, vmem_limit_bytes=(60 * 1024 - 256) * 1024
         ),
     )(embeddings, labels.reshape(1, rows), order, head_weight)
 

time: 42 us -> 40.8 us (0.971)
  local copies, waits for them, and re-layouts: 4.24 us -> 2.42 us
  Pallas kernels: 37 us -> 37.5 us
    unnamed x10 -> x4, local copies, waits for them, and re-layouts: 4.24 us -> 2.42 us
    pallas_call x1, Pallas kernels: 37 us -> 37.5 us  [body(): pl.pallas_call(functools.partial(kernel, m), out_shape=(jax.ShapeDtypeStr...]
where the time goes in v5:
time: 40.8 us; the launch traced here: 40.6 us
  Pallas kernels  37.5 us (92%)
  local copies, waits for them, and re-layouts  2.42 us (6%)
  between operations  0.65 us (2%)
    pallas_call x1, Pallas kernels, body(): pl.pallas_call(functools.partial(kernel, m), out_shape=(jax.ShapeDtypeStr...  37.5 us
    unnamed x4, local copies, waits for them, and re-layouts  2.42 us

profile of v5, /device:TPU:0, one launch (start us, length us, event | category | flops | bytes accessed | tf_op | source)
XLA Modules:
  0.0 40.6 jit_solution(6187688668144617775)
XLA Ops:
  0.6 37.5 %shard_map.59 = (bf16[128,1024]{1,0:T(8,128)(2,1)}, f32[128,512]{1,0:T(8,128)}) custom-call(bf16[128,1024]{1,0:T(8,128)(2,1)} %emb_hbm.1, s32[1,128]{1,0:T(1,128)} %bitcast.1, s32[1,128]{1,0:T(1,128)} %order_hbm.1, bf16[1024,512]{1,0:T(8,128)(2,1)} %head_hbm.1), custom_call_target="tpu_custom_call" | custom-call | flops 671088640 | bytes 1572864 | tf_op jit(solution)/shard_map/pallas_call | solution.py:384
  38.2 0.0 copy-start
  38.2 1.7 %copy.8 = bf16[128,1024]{1,0:T(8,128)(2,1)} copy(bf16[128,1024]{1,0:T(8,128)(2,1)} %get-tuple-element.4) | data formatting | bytes 524288
  39.9 0.0 copy-done
  39.9 0.7 %copy.9 = f32[128,512]{1,0:T(8,128)} copy(f32[128,512]{1,0:T(8,128)S(1)} %copy-done) | data formatting | bytes 524288
Async XLA Ops:
  38.2 1.7 %copy-start = (f32[128,512]{1,0:T(8,128)S(1)}, f32[128,512]{1,0:T(8,128)}, u32[]{:S(2)}) copy-start(f32[128,512]{1,0:T(8,128)} %get-tuple-element.5) | copy-start | bytes 786436

commit v6 on v5

--- a/solution.py
+++ b/solution.py
@@ -392,7 +392,7 @@
         scratch_shapes=scratch,
         cost_estimate=pl.CostEstimate(flops=2 * macs, bytes_accessed=4 * rows * width + 2 * width * proj, transcendentals=rows * rows * nk),
         compiler_params=pltpu.CompilerParams(
-            collective_id=0, has_side_effects=True, vmem_limit_bytes=(60 * 1024 - 256) * 1024
+            collective_id=0, has_side_effects=True, vmem_limit_bytes=(60 * 1024 - 640) * 1024
         ),
     )(embeddings, labels.reshape(1, rows), order, head_weight)
 

time: 40.8 us -> 40.8 us (level)
  no operation moved by 1% of the time
where the time goes in v6:
time: 40.8 us; the launch traced here: 40.6 us
  Pallas kernels  37.5 us (92%)
  local copies, waits for them, and re-layouts  2.42 us (6%)
  between operations  0.65 us (2%)
    pallas_call x1, Pallas kernels, body(): pl.pallas_call(functools.partial(kernel, m), out_shape=(jax.ShapeDtypeStr...  37.5 us
    unnamed x4, local copies, waits for them, and re-layouts  2.42 us

profile of v6, /device:TPU:0, one launch (start us, length us, event | category | flops | bytes accessed | tf_op | source)
XLA Modules:
  0.0 40.6 jit_solution(6187688668144617775)
XLA Ops:
  0.6 37.5 %shard_map.59 = (bf16[128,1024]{1,0:T(8,128)(2,1)}, f32[128,512]{1,0:T(8,128)}) custom-call(bf16[128,1024]{1,0:T(8,128)(2,1)} %emb_hbm.1, s32[1,128]{1,0:T(1,128)} %bitcast.1, s32[1,128]{1,0:T(1,128)} %order_hbm.1, bf16[1024,512]{1,0:T(8,128)(2,1)} %head_hbm.1), custom_call_target="tpu_custom_call" | custom-call | flops 671088640 | bytes 1572864 | tf_op jit(solution)/shard_map/pallas_call | solution.py:384
  38.2 0.0 copy-start
  38.2 1.7 %copy.8 = bf16[128,1024]{1,0:T(8,128)(2,1)} copy(bf16[128,1024]{1,0:T(8,128)(2,1)} %get-tuple-element.4) | data formatting | bytes 524288
  39.9 0.0 copy-done
  39.9 0.7 %copy.9 = f32[128,512]{1,0:T(8,128)} copy(f32[128,512]{1,0:T(8,128)S(1)} %copy-done) | data formatting | bytes 524288
Async XLA Ops:
  38.2 1.7 %copy-start = (f32[128,512]{1,0:T(8,128)S(1)}, f32[128,512]{1,0:T(8,128)}, u32[]{:S(2)}) copy-start(f32[128,512]{1,0:T(8,128)} %get-tuple-element.5) | copy-start | bytes 786436

commit v7 on v6

--- a/solution.py
+++ b/solution.py
@@ -392,7 +392,7 @@
         scratch_shapes=scratch,
         cost_estimate=pl.CostEstimate(flops=2 * macs, bytes_accessed=4 * rows * width + 2 * width * proj, transcendentals=rows * rows * nk),
         compiler_params=pltpu.CompilerParams(
-            collective_id=0, has_side_effects=True, vmem_limit_bytes=(60 * 1024 - 640) * 1024
+            collective_id=0, has_side_effects=True, vmem_limit_bytes=59 * 1024 * 1024
         ),
     )(embeddings, labels.reshape(1, rows), order, head_weight)
 

time: 40.8 us -> 40.8 us (level)
  no operation moved by 1% of the time
where the time goes in v7:
time: 40.8 us; the launch traced here: 40.6 us
  Pallas kernels  37.5 us (92%)
  local copies, waits for them, and re-layouts  2.42 us (6%)
  between operations  0.65 us (2%)
    pallas_call x1, Pallas kernels, body(): pl.pallas_call(functools.partial(kernel, m), out_shape=(jax.ShapeDtypeStr...  37.5 us
    unnamed x4, local copies, waits for them, and re-layouts  2.42 us

profile of v7, /device:TPU:0, one launch (start us, length us, event | category | flops | bytes accessed | tf_op | source)
XLA Modules:
  0.0 40.6 jit_solution(6187688668144617775)
XLA Ops:
  0.6 37.5 %shard_map.59 = (bf16[128,1024]{1,0:T(8,128)(2,1)}, f32[128,512]{1,0:T(8,128)}) custom-call(bf16[128,1024]{1,0:T(8,128)(2,1)} %emb_hbm.1, s32[1,128]{1,0:T(1,128)} %bitcast.1, s32[1,128]{1,0:T(1,128)} %order_hbm.1, bf16[1024,512]{1,0:T(8,128)(2,1)} %head_hbm.1), custom_call_target="tpu_custom_call" | custom-call | flops 671088640 | bytes 1572864 | tf_op jit(solution)/shard_map/pallas_call | solution.py:384
  38.2 0.0 copy-start
  38.2 1.7 %copy.8 = bf16[128,1024]{1,0:T(8,128)(2,1)} copy(bf16[128,1024]{1,0:T(8,128)(2,1)} %get-tuple-element.4) | data formatting | bytes 524288
  39.9 0.0 copy-done
  39.9 0.7 %copy.9 = f32[128,512]{1,0:T(8,128)} copy(f32[128,512]{1,0:T(8,128)S(1)} %copy-done) | data formatting | bytes 524288
Async XLA Ops:
  38.2 1.7 %copy-start = (f32[128,512]{1,0:T(8,128)S(1)}, f32[128,512]{1,0:T(8,128)}, u32[]{:S(2)}) copy-start(f32[128,512]{1,0:T(8,128)} %get-tuple-element.5) | copy-start | bytes 786436
